TPU v7x, 32 devices: a whole 2x2x4 slice. The times are simulated.
32 devices in a mesh: users: 8 (over y, x, core), items: 4 (over z).
Axes of the slice: x: 2, y: 2, z: 4, core: 2. Of those that a mesh axis runs over, the one named last changes fastest.
Arguments:
- user_factors: float32 [16384, 128], P('users'), may hold values from -1.8 to 1.8
- user_moment_one: float32 [16384, 128], P('users'), may hold values from -1.8 to 1.8
- user_moment_two: float32 [16384, 128], P('users'), may hold values from 0.01 to 1
- item_factors: float32 [6144, 128], P(('items', 'users')), may hold values from -1.8 to 1.8
- item_moment_one: float32 [6144, 128], P(('items', 'users')), may hold values from -1.8 to 1.8
- item_moment_two: float32 [6144, 128], P(('items', 'users')), may hold values from 0.01 to 1
- block_slot: int32 [8, 4, 128], P('users', 'items'), may hold values from 0 to 191, as said below
- block_count: int32 [8, 4], P('users', 'items'), may hold values from 32 to 128, as said below
- block_values: bfloat16 [8, 4, 128, 128, 128], P('users', 'items'), may hold values from 0 to 4
Outputs:
- new_user_factors: float32 [16384, 128], P(('users', 'items'))
- new_user_moment_one: float32 [16384, 128], P(('users', 'items'))
- new_user_moment_two: float32 [16384, 128], P(('users', 'items'))
- new_item_factors: float32 [6144, 128], P(('items', 'users'))
- new_item_moment_one: float32 [6144, 128], P(('items', 'users'))
- new_item_moment_two: float32 [6144, 128], P(('items', 'users'))
Inputs may be any that keep to these rules, and one draw needn't show every extreme that they name: `block_slot`: in every grid cell the 128 entries are distinct. `block_count`: some grid cell has exactly 128 live blocks.
All inputs are finite; a program needn't handle non-finite values.
Results may differ from a plain program's by a relative error of at most 0.0046.
Values may be sent and summed in bfloat16 or wider, within the bound.
A program may use at most 64 MiB of HBM per device.

v0:
```python
import math

import jax
import jax.numpy as jnp
from jax import lax
from jax.sharding import PartitionSpec as P

conf_alpha = 0.5
reg_weight = 0.5
beta_one = 0.9
beta_two = 0.95
learn_rate = 0.1
adam_eps = 1e-08
correction_one = 1.0 - beta_one**11
correction_two = 1.0 - beta_two**11


def adam_update(parameter, first_moment, second_moment, grad_sum, grad_scale):
    gradient = grad_sum * grad_scale + reg_weight * parameter
    first_new = beta_one * first_moment + (1.0 - beta_one) * gradient
    second_new = beta_two * second_moment + (1.0 - beta_two) * gradient * gradient
    step_size = first_new / correction_one / (jnp.sqrt(second_new / correction_two) + adam_eps)
    return (parameter - learn_rate * step_size, first_new, second_new)


def weighted_error(predicted, block_vals, live_mask):
    target = block_vals.astype(jnp.float32)
    return jnp.where(live_mask, (1.0 + conf_alpha * target) * (predicted - target), 0.0).astype(
        jnp.bfloat16
    )


def build_tile(slot_list, live_count, block_vals, user_blocks, item_blocks):
    capacity = slot_list.shape[0]
    block_edge = block_vals.shape[-1]
    tile_slots = user_blocks * item_blocks
    live_mask = jnp.arange(capacity, dtype=jnp.int32) < live_count
    target_slot = jnp.where(live_mask, slot_list, tile_slots)
    tile_values = (
        jnp.zeros((tile_slots, block_edge, block_edge), jnp.bfloat16)
        .at[target_slot]
        .set(block_vals, mode="drop")
    )
    tile_live = jnp.zeros((tile_slots,), jnp.bool_).at[target_slot].set(True, mode="drop")
    return (
        tile_values.reshape(user_blocks, item_blocks, block_edge, block_edge),
        tile_live.reshape(user_blocks, item_blocks),
    )


def dense_pass(user_panel, item_panel, tile_values, tile_live, toward_users):

    def advance(running, inputs):
        user_row, row_values, row_live = inputs
        predicted = jnp.einsum(
            "ar,ibr->iab", user_row, item_panel, preferred_element_type=jnp.float32
        )
        weighted = weighted_error(predicted, row_values, row_live[:, None, None])
        if toward_users:
            return (
                running,
                jnp.einsum("iab,ibr->ar", weighted, item_panel, preferred_element_type=jnp.float32),
            )
        return (
            running
            + jnp.einsum("iab,ar->ibr", weighted, user_row, preferred_element_type=jnp.float32),
            None,
        )

    running, user_rows = lax.scan(
        advance, jnp.zeros(item_panel.shape, jnp.float32), (user_panel, tile_values, tile_live)
    )
    if toward_users:
        return user_rows
    return running


def on_device(
    user_factors,
    user_moment_one,
    user_moment_two,
    item_factors,
    item_moment_one,
    item_moment_two,
    block_slot,
    block_count,
    block_values,
):
    slot_list = block_slot[0, 0]
    live_count = block_count[0, 0]
    values_here = block_values[0, 0]
    rank = user_factors.shape[1]
    block_edge = values_here.shape[-1]
    gathered = lax.all_gather(item_factors.astype(jnp.bfloat16), "users", axis=0, tiled=True)
    item_panel = gathered.reshape(-1, block_edge, rank)
    user_panel = user_factors.astype(jnp.bfloat16).reshape(-1, block_edge, rank)
    item_total = item_panel.shape[0] * block_edge * lax.axis_size("items")
    user_total = user_factors.shape[0] * lax.axis_size("users")
    tile_values, tile_live = build_tile(
        slot_list, live_count, values_here, user_panel.shape[0], item_panel.shape[0]
    )
    user_partial = dense_pass(user_panel, item_panel, tile_values, tile_live, True)
    user_partial = user_partial.reshape(-1, rank)
    user_share = user_factors.shape[0] // lax.axis_size("items")
    user_offset = lax.axis_index("items") * user_share
    user_sum = lax.psum(user_partial, "items")
    new_user, new_user_one, new_user_two = adam_update(
        user_factors, user_moment_one, user_moment_two, user_sum, 1.0 / math.sqrt(item_total)
    )
    new_low = new_user.astype(jnp.bfloat16)
    new_user = lax.dynamic_slice_in_dim(new_user, user_offset, user_share, 0)
    new_user_one = lax.dynamic_slice_in_dim(new_user_one, user_offset, user_share, 0)
    new_user_two = lax.dynamic_slice_in_dim(new_user_two, user_offset, user_share, 0)
    new_panel = new_low.reshape(-1, block_edge, rank)
    item_partial = dense_pass(new_panel, item_panel, tile_values, tile_live, False)
    item_partial = item_partial.reshape(-1, rank)
    item_whole_sum = lax.psum(item_partial, "users")
    item_share = item_factors.shape[0]
    item_sum = lax.dynamic_slice_in_dim(
        item_whole_sum, lax.axis_index("users") * item_share, item_share, 0
    )
    new_item, new_item_one, new_item_two = adam_update(
        item_factors, item_moment_one, item_moment_two, item_sum, 1.0 / math.sqrt(user_total)
    )
    return (new_user, new_user_one, new_user_two, new_item, new_item_one, new_item_two)


def solution(mesh):
    return jax.shard_map(
        on_device,
        mesh=mesh,
        in_specs=(
            P("users", None),
            P("users", None),
            P("users", None),
            P(("items", "users"), None),
            P(("items", "users"), None),
            P(("items", "users"), None),
            P("users", "items", None),
            P("users", "items"),
            P("users", "items", None, None, None),
        ),
        out_specs=(
            P(("users", "items"), None),
            P(("users", "items"), None),
            P(("users", "items"), None),
            P(("items", "users"), None),
            P(("items", "users"), None),
            P(("items", "users"), None),
        ),
        check_vma=False,
    )
```

profile of v0, /device:TPU:0, one launch (start us, length us, event | category | flops | bytes accessed | tf_op | source)
XLA Modules:
  0.0 244.7 jit_solution(2892566918279856874)
XLA Ops:
  7.9 0.7 fusion.50
  8.5 1.0 scatter_custom_fusion
  9.6 0.9 convert_element_type.28
  10.5 11.0 %all_gather.3 = bf16[1536,128]{1,0:T(8,128)(2,1)S(1)} all-gather(bf16[192,128]{1,0:T(8,128)(2,1)S(1)} %convert_element_type.28), channel_id=1, replica_groups=mesh['users'=8,'items'=4] {'users'}, dimensions={0}, use_global_device_ids=true | all-gather | bytes 442368 | tf_op jit(solution)/shard_map/all_gather | solution.py:94
  21.6 1.3 convert_element_type.27
  22.9 4.2 %broadcast_in_dim.55 = bf16[192,128,128]{2,1,0:T(8,128)(2,1)} broadcast(bf16[]{:T(256)} %constant.49.clone.1), dimensions={} | broadcast | bytes 6291458 | tf_op jit(solution)/shard_map/broadcast_in_dim | solution.py:40
  27.1 19.5 %scatter_fusion = bf16[192,128,128]{2,1,0:T(8,128)(2,1)} fusion(bf16[192,128,128]{2,1,0:T(8,128)(2,1)} %broadcast_in_dim.55, s32[128]{0:T(128)S(1)} %fusion.50, bf16[128,128,128]{2,1,0:T(8,128)(2,1)} %bitcast.106), kind=kCustom, calls=%fused_computation.1 | custom fusion | bytes 12583424 | tf_op jit(solution)/shard_map/scatter | solution.py:42
  46.6 33.2 %while.21 = (s32[]{:T(128)}, f32[16,128,128]{2,1,0:T(8,128)}, pred[16,12]{1,0:T(8,128)(4,1)S(1)}, bf16[16,12,128,128]{3,2,1,0:T(8,128)(2,1)}, bf16[16,128,128]{2...) while((s32[]{:T(128)}, f32[16,128,128]{2,1,0:T(8,128)}, pred[16,12]{1,0:T(8,128)(4,1)S(1)}, ...), condition=%wide.region_3.4_spmd, body=%wide.region_2.3_spmd.sunk | while | flops 102039552 | bytes 1280105 | solution.py:70
  46.6 2.1 fusion.67
  48.8 2.1 fusion.67
  50.8 2.1 fusion.67
  52.9 2.1 fusion.67
  55.0 2.1 fusion.67
  57.0 2.1 fusion.67
  59.1 2.0 fusion.67
  61.2 2.1 fusion.67
  63.2 2.1 fusion.67
  65.3 2.1 fusion.67
  67.4 2.1 fusion.67
  69.4 2.1 fusion.67
  71.5 2.1 fusion.67
  73.6 2.1 fusion.67
  75.6 2.1 fusion.67
  77.7 2.1 fusion.67
  79.9 52.3 %all-reduce.3.cloned.1.call-done = f32[2048,128]{1,0:T(8,128)} async-done(((f32[2048,128]{1,0:T(8,128)}), f32[2048,128]{1,0:T(8,128)}) %all-reduce.3.cloned.1.call-update) | async-done | bytes 1048592 | tf_op jit(solution)/shard_map/psum | solution.py:106
  132.2 3.9 %fusion.52 = (bf16[2048,128]{1,0:T(8,128)(2,1)}, f32[2048,128]{1,0:T(8,128)S(1)}, f32[2048,128]{1,0:T(8,128)}, f32[2048,128]{1,0:T(8,128)}) fusion(f32[2048,128]{1,0:T(8,128)S(1)} %copy-done.1, f32[2048,128]{1,0:T(8,128)} %all-reduce.3.cloned.1.call-done, f32[2048,128]{1,0:T(8,128)} %param.14, f32[2048,128]{1,0:T(8,128)} %param.15), kind=kLoop, calls=%fused_computation.66 | loop fusion | flops 4456448 | bytes 7864320 | tf_op jit(solution)/shard_map/convert_element_type | solution.py:110
  136.1 44.2 %while.22 = (s32[]{:T(128)}, f32[12,128,128]{2,1,0:T(8,128)S(1)}, pred[16,12]{1,0:T(8,128)(4,1)S(1)}, bf16[16,12,128,128]{3,2,1,0:T(8,128)(2,1)}, bf16[16,128,12...) while((s32[]{:T(128)}, f32[12,128,128]{2,1,0:T(8,128)S(1)}, ...), condition=%wide.region_6.7_spmd.clone, body=%wide.region_5.6_spmd.clone.sunk | while | flops 102432768 | bytes 3998859 | solution.py:70
  136.1 1.1 constant_dynamic-slice_fusion.5
  137.4 1.4 convolution_add_fusion.2
  138.9 1.0 constant_dynamic-slice_fusion.5
  140.2 1.4 convolution_add_fusion.2
  141.7 1.0 constant_dynamic-slice_fusion.5
  143.0 1.4 convolution_add_fusion.2
  144.4 1.0 constant_dynamic-slice_fusion.5
  145.7 1.4 convolution_add_fusion.2
  147.2 1.0 constant_dynamic-slice_fusion.5
  148.5 1.4 convolution_add_fusion.2
  149.9 1.0 constant_dynamic-slice_fusion.5
  151.2 1.4 convolution_add_fusion.2
  152.7 1.0 constant_dynamic-slice_fusion.5
  154.0 1.4 convolution_add_fusion.2
  155.5 1.0 constant_dynamic-slice_fusion.5
  156.7 1.4 convolution_add_fusion.2
  158.2 1.0 constant_dynamic-slice_fusion.5
  159.5 1.4 convolution_add_fusion.2
  161.0 1.0 constant_dynamic-slice_fusion.5
  162.3 1.4 convolution_add_fusion.2
  163.7 1.0 constant_dynamic-slice_fusion.5
  165.0 1.4 convolution_add_fusion.2
  166.5 1.0 constant_dynamic-slice_fusion.5
  167.8 1.4 convolution_add_fusion.2
  169.2 1.0 constant_dynamic-slice_fusion.5
  170.5 1.4 convolution_add_fusion.2
  172.0 1.0 constant_dynamic-slice_fusion.5
  173.3 1.4 convolution_add_fusion.2
  174.8 1.0 constant_dynamic-slice_fusion.5
  176.0 1.4 convolution_add_fusion.2
  177.5 1.0 constant_dynamic-slice_fusion.5
  178.8 1.4 convolution_add_fusion.2
  180.3 0.9 copy-done
  181.2 0.7 constant_dynamic-slice_fusion.3
  181.9 1.9 constant_dynamic-slice_fusion.1
  183.8 52.5 %all-reduce.5.cloned.1.call-done = f32[1536,128]{1,0:T(8,128)} async-done(((f32[1536,128]{1,0:T(8,128)}), f32[1536,128]{1,0:T(8,128)}) %all-reduce.5.cloned.1.call-update) | async-done | bytes 786448 | tf_op jit(solution)/shard_map/psum | solution.py:117
  236.3 1.6 multiply_subtract_fusion.1
  (65 shorter events, 4.3 us)
Async XLA Ops:
  7.2 125.0 %all-reduce.3.cloned.1.call-start = ((), (), s32[]{:S(2)}) async-start(), calls=%async_computation | async-start | bytes 2097152 | tf_op jit(solution)/shard_map/psum | solution.py:106
  46.6 85.6 %copy-start.1 = (f32[2048,128]{1,0:T(8,128)S(1)}, f32[2048,128]{1,0:T(8,128)}, u32[]{:S(2)}) copy-start(f32[2048,128]{1,0:T(8,128)} %param.13) | copy-start | bytes 3145732
  79.8 156.5 %all-reduce.5.cloned.1.call-start = ((), (), s32[]{:S(2)}) async-start(), calls=%async_computation.1 | async-start | bytes 1572864 | tf_op jit(solution)/shard_map/psum | solution.py:117
  136.1 100.1 %copy-start.2 = (f32[192,128]{1,0:T(8,128)S(1)}, f32[192,128]{1,0:T(8,128)}, u32[]{:S(2)}) copy-start(f32[192,128]{1,0:T(8,128)} %param.16) | copy-start | bytes 294916
  136.1 100.1 %copy-start.3 = (f32[192,128]{1,0:T(8,128)S(1)}, f32[192,128]{1,0:T(8,128)}, u32[]{:S(2)}) copy-start(f32[192,128]{1,0:T(8,128)} %param.17) | copy-start | bytes 294916
  136.1 100.1 %copy-start.4 = (f32[192,128]{1,0:T(8,128)S(1)}, f32[192,128]{1,0:T(8,128)}, u32[]{:S(2)}) copy-start(f32[192,128]{1,0:T(8,128)} %param.18) | copy-start | bytes 294916
  180.3 0.9 copy-start
Sparse Core Ops, SparseCore 0:
  79.9 52.2 all-reduce.2
  181.3 54.8 all-reduce.4
where the time goes:
time: 248 us; the launch traced here: 245 us
  waiting for transfers between devices  105 us (42%)
  matrix products  56.1 us (23%)
  local copies, waits for them, and re-layouts  48.8 us (20%)
  between operations  14.8 us (6%)
  blocking collectives  11 us (4%)
  other arithmetic  8.41 us (3%)
    psum x1, waiting for transfers between devices, on_device(): item_whole_sum = lax.psum(item_partial, 'users')  52.5 us
    psum x1, waiting for transfers between devices, on_device(): user_sum = lax.psum(user_partial, 'items')  52.3 us
    dot_general x16, matrix products, advance(): jnp.einsum('iab,ibr->ar', weighted, item_panel, preferred_element_type=jn...  33 us
    dot_general x16, matrix products, advance(): jnp.einsum('iab,ar->ibr', weighted, user_row, preferred_element_type=jnp....  23.1 us
    dynamic_slice x32, local copies, waits for them, and re-layouts, dense_pass(): lax.scan(advance, jnp.zeros(item_panel.shape, jnp.float32), (user_panel,...  20.1 us
    scatter x1, local copies, waits for them, and re-layouts, build_tile(): tile_values = jnp.zeros((tile_slots, block_edge, block_edge), jnp.bfloat1...  19.5 us
    all_gather x1, blocking collectives, on_device(): lax.all_gather(item_factors.astype(jnp.bfloat16), 'users', axis=0, tiled=...  11 us
  transfers between devices with their start and end apart: 2, of which 2 were waited for; matrix products, arithmetic and copies ran while one was open for 1% of the time, Pallas kernels for 0%

commit v1 on v0

v1 whole, which is shorter than its diff:
```python
import functools
import math

import jax
import jax.numpy as jnp
from jax import lax
from jax.experimental import pallas as pl
from jax.experimental.pallas import tpu as pltpu
from jax.sharding import PartitionSpec as P

conf_alpha = 0.5
reg_weight = 0.5
beta_one = 0.9
beta_two = 0.95
learn_rate = 0.1
adam_eps = 1e-08
correction_one = 1.0 - beta_one**11
correction_two = 1.0 - beta_two**11

f32, bf16 = jnp.float32, jnp.bfloat16


def adam_update(parameter, first_moment, second_moment, grad_sum, grad_scale):
    gradient = grad_sum * grad_scale + reg_weight * parameter
    first_new = beta_one * first_moment + (1.0 - beta_one) * gradient
    second_new = beta_two * second_moment + (1.0 - beta_two) * gradient * gradient
    step_size = first_new / correction_one / (jnp.sqrt(second_new / correction_two) + adam_eps)
    return (parameter - learn_rate * step_size, first_new, second_new)


def find_blocks(slot_list, live_count, slots):
    places = jnp.arange(slot_list.shape[0], dtype=jnp.int32)
    here = (slot_list[None, :] == jnp.arange(slots, dtype=jnp.int32)[:, None]) & (
        places < live_count
    )[None, :]
    return jnp.max(jnp.where(here, places[None, :], -1), axis=1)


def kernel(
    n_users, n_items, edge,
    place, uf_hbm, um1_hbm, um2_hbm, if_hbm, im1_hbm, im2_hbm, vals_hbm,
    nu_hbm, nu1_hbm, nu2_hbm, ni_hbm, ni1_hbm, ni2_hbm,
    vals, uf, um1, um2, itf, im1, im2, u_low, panel, item_t,
    acc, send_u, recv_u, new_low, item_acc, item_sum, item_send, recv_i,
    load_sem, store_sem, gs_sem, gr_sem, us_sem, ur_sem, as_sem, ar_sem, is_sem, ir_sem,
):
    me_u, me_i = lax.axis_index("users"), lax.axis_index("items")
    user_rows, rank = uf.shape
    item_rows = panel.shape[0]
    user_share, item_share = user_rows // n_items, item_rows // n_users
    share_blocks, item_blocks = user_share // edge, item_rows // edge
    width = 2 if item_blocks % 2 == 0 else 1
    pairs = item_blocks // width
    span = width * edge

    def u_share(j):
        return pl.ds(pl.multiple_of(j * user_share, user_share), user_share)

    def i_share(j):
        return pl.ds(pl.multiple_of(j * item_share, item_share), item_share)

    def to(src, dst, s_sem, r_sem, axis, j):
        return pltpu.make_async_remote_copy(
            src_ref=src, dst_ref=dst, send_sem=s_sem, recv_sem=r_sem,
            device_id={axis: j}, device_id_type=pl.DeviceIdType.MESH,
        )

    def user_peers(body):
        def step(t, carry):
            body(lax.rem(me_u + t, n_users))
            return carry

        lax.fori_loop(1, n_users, step, 0)

    def item_peers(body):
        def step(t, carry):
            body(lax.rem(me_i + t, n_items))
            return carry

        lax.fori_loop(1, n_items, step, 0)

    own = u_share(me_i)
    loads = [
        pltpu.make_async_copy(src, dst, load_sem.at[n])
        for n, (src, dst) in enumerate(
            (
                (if_hbm, itf), (uf_hbm, uf), (vals_hbm, vals),
                (um1_hbm.at[own], um1), (um2_hbm.at[own], um2),
                (im1_hbm, im1), (im2_hbm, im2),
            )
        )
    ]
    for load in loads:
        load.start()

    barrier = pltpu.get_barrier_semaphore()

    def greet_user(j):
        pl.semaphore_signal(
            barrier, inc=1, device_id={"users": j}, device_id_type=pl.DeviceIdType.MESH
        )

    def greet_item(j):
        pl.semaphore_signal(
            barrier, inc=1, device_id={"items": j}, device_id_type=pl.DeviceIdType.MESH
        )

    user_peers(greet_user)
    item_peers(greet_item)
    loads[0].wait()
    panel[i_share(me_u), :] = itf[...].astype(bf16)
    pl.semaphore_wait(barrier, n_users + n_items - 2)

    def gather(j):
        mine = panel.at[i_share(me_u)]
        return to(mine, mine, gs_sem.at[j], gr_sem.at[me_u], "users", j)

    def gathered(j):
        theirs = panel.at[i_share(j)]
        return to(theirs, theirs, gs_sem.at[j], gr_sem.at[j], "users", j)

    user_peers(lambda j: gather(j).start())
    loads[1].wait()
    u_low[...] = uf[...].astype(bf16)
    loads[2].wait()
    user_peers(lambda j: gathered(j).wait_recv())
    for b in range(item_blocks):
        item_t[:, b * edge : (b + 1) * edge] = panel[b * edge : (b + 1) * edge, :].T

    def errors(rows, first_block, p):
        cols = item_t[:, pl.ds(pl.multiple_of(p * span, span), span)]
        predicted = jnp.dot(rows, cols, preferred_element_type=f32)
        strips = []
        for ub in range(share_blocks):
            parts = []
            for h in range(width):
                k = place[(first_block + ub) * item_blocks + p * width + h]
                live = jnp.where(k < 0, 0.0, 1.0).astype(f32)
                y = vals[jnp.maximum(k, 0)].astype(f32)
                pred = predicted[ub * edge : (ub + 1) * edge, h * edge : (h + 1) * edge]
                parts.append(((live + (conf_alpha * live) * y) * (pred - y)).astype(bf16))
            strips.append(jnp.concatenate(parts, axis=1))
        return jnp.concatenate(strips, axis=0)

    def send_share(j):
        return to(send_u.at[j], recv_u.at[me_i], us_sem.at[j], ur_sem.at[me_i], "items", j)

    def first_pass(t, carry):
        j = lax.rem(me_i + 1 + t, n_items)
        acc[...] = jnp.zeros_like(acc)

        def step(p, c):
            rows = u_low[u_share(j), :]
            weighted = errors(rows, j * share_blocks, p)
            it = panel[pl.ds(pl.multiple_of(p * span, span), span), :]
            acc[...] += jnp.dot(weighted, it, preferred_element_type=f32)
            return c

        lax.fori_loop(0, pairs, step, 0)

        @pl.when(t < n_items - 1)
        def _():
            send_u[j] = acc[...].astype(bf16)
            send_share(j).start()

        return carry

    lax.fori_loop(0, n_items, first_pass, 0)
    loads[3].wait()
    loads[4].wait()

    def add_share(j):
        to(
            send_u.at[j], recv_u.at[j], us_sem.at[j], ur_sem.at[j], "items", j
        ).wait_recv()
        acc[...] += recv_u[j].astype(f32)

    item_peers(add_share)
    user_scale = 1.0 / math.sqrt(item_rows * n_items)
    new, one, two = adam_update(uf[own, :], um1[...], um2[...], acc[...], user_scale)
    new_low[own, :] = new.astype(bf16)

    def spread(j):
        mine = new_low.at[own]
        return to(mine, mine, as_sem.at[j], ar_sem.at[me_i], "items", j)

    item_peers(lambda j: spread(j).start())
    acc[...] = new
    um1[...] = one
    um2[...] = two
    stores = [
        pltpu.make_async_copy(src, dst, store_sem.at[n])
        for n, (src, dst) in enumerate(
            (
                (acc, nu_hbm), (um1, nu1_hbm), (um2, nu2_hbm),
                (itf, ni_hbm), (im1, ni1_hbm), (im2, ni2_hbm),
            )
        )
    ]
    for store in stores[:3]:
        store.start()

    item_acc[...] = jnp.zeros_like(item_acc)

    def second_pass(t, carry):
        j = lax.rem(me_i + t, n_items)

        @pl.when(t > 0)
        def _():
            theirs = new_low.at[u_share(j)]
            to(theirs, theirs, as_sem.at[j], ar_sem.at[j], "items", j).wait_recv()

        rows_t = jnp.concatenate(
            [
                new_low[pl.ds(pl.multiple_of((j * share_blocks + b) * edge, edge), edge), :].T
                for b in range(share_blocks)
            ],
            axis=1,
        )

        def step(p, c):
            rows = new_low[u_share(j), :]
            weighted = errors(rows, j * share_blocks, p)
            cols = pl.ds(pl.multiple_of(p * span, span), span)
            item_acc[:, cols] += jnp.dot(rows_t, weighted, preferred_element_type=f32)
            return c

        lax.fori_loop(0, pairs, step, 0)
        return carry

    lax.fori_loop(0, n_items, second_pass, 0)
    for b in range(item_blocks):
        tile = item_acc[:, b * edge : (b + 1) * edge].T
        item_sum[b * edge : (b + 1) * edge, :] = tile
        item_send[b * edge : (b + 1) * edge, :] = tile.astype(bf16)

    def send_items(j):
        return to(
            item_send.at[i_share(j)], recv_i.at[me_u],
            is_sem.at[j], ir_sem.at[me_u], "users", j,
        )

    user_peers(lambda j: send_items(j).start())
    loads[5].wait()
    loads[6].wait()

    def add_items(j):
        to(
            item_send.at[i_share(j)], recv_i.at[j], is_sem.at[j], ir_sem.at[j], "users", j
        ).wait_recv()
        item_sum[i_share(me_u), :] += recv_i[j].astype(f32)

    user_peers(add_items)
    item_scale = 1.0 / math.sqrt(user_rows * n_users)
    new, one, two = adam_update(
        itf[...], im1[...], im2[...], item_sum[i_share(me_u), :], item_scale
    )
    itf[...] = new
    im1[...] = one
    im2[...] = two
    for store in stores[3:]:
        store.start()

    user_peers(lambda j: gather(j).wait_send())
    user_peers(lambda j: send_items(j).wait_send())
    item_peers(lambda j: send_share(j).wait_send())
    item_peers(lambda j: spread(j).wait_send())
    for store in stores:
        store.wait()


def on_device(
    n_users, n_items,
    user_factors, user_moment_one, user_moment_two,
    item_factors, item_moment_one, item_moment_two,
    block_slot, block_count, block_values,
):
    values = block_values[0, 0]
    edge = values.shape[-1]
    user_rows, rank = user_factors.shape
    item_share = item_factors.shape[0]
    item_rows = item_share * n_users
    user_share = user_rows // n_items
    slots = (user_rows // edge) * (item_rows // edge)
    place = find_blocks(block_slot[0, 0], block_count[0, 0], slots)
    vm = pltpu.VMEM
    dma = pltpu.SemaphoreType.DMA
    user_out = jax.ShapeDtypeStruct((user_share, rank), f32)
    item_out = jax.ShapeDtypeStruct((item_share, rank), f32)
    anywhere = pl.BlockSpec(memory_space=pl.ANY)
    return pl.pallas_call(
        functools.partial(kernel, n_users, n_items, edge),
        out_shape=(user_out,) * 3 + (item_out,) * 3,
        in_specs=[pl.BlockSpec(memory_space=pltpu.SMEM)] + [anywhere] * 7,
        out_specs=(anywhere,) * 6,
        scratch_shapes=[
            vm(values.shape, bf16),
            vm((user_rows, rank), f32),
            vm((user_share, rank), f32),
            vm((user_share, rank), f32),
            vm((item_share, rank), f32),
            vm((item_share, rank), f32),
            vm((item_share, rank), f32),
            vm((user_rows, rank), bf16),
            vm((item_rows, rank), bf16),
            vm((rank, item_rows), bf16),
            vm((user_share, rank), f32),
            vm((n_items, user_share, rank), bf16),
            vm((n_items, user_share, rank), bf16),
            vm((user_rows, rank), bf16),
            vm((rank, item_rows), f32),
            vm((item_rows, rank), f32),
            vm((item_rows, rank), bf16),
            vm((n_users, item_share, rank), bf16),
            dma((7,)),
            dma((6,)),
            dma((n_users,)),
            dma((n_users,)),
            dma((n_items,)),
            dma((n_items,)),
            dma((n_items,)),
            dma((n_items,)),
            dma((n_users,)),
            dma((n_users,)),
        ],
        compiler_params=pltpu.CompilerParams(
            collective_id=0, has_side_effects=True, vmem_limit_bytes=56 * 2**20
        ),
        name="factorization_step",
    )(
        place, user_factors, user_moment_one, user_moment_two,
        item_factors, item_moment_one, item_moment_two, values,
    )


def solution(mesh):
    return jax.shard_map(
        functools.partial(on_device, mesh.shape["users"], mesh.shape["items"]),
        mesh=mesh,
        in_specs=(
            P("users", None),
            P("users", None),
            P("users", None),
            P(("items", "users"), None),
            P(("items", "users"), None),
            P(("items", "users"), None),
            P("users", "items", None),
            P("users", "items"),
            P("users", "items", None, None, None),
        ),
        out_specs=(
            P(("users", "items"), None),
            P(("users", "items"), None),
            P(("users", "items"), None),
            P(("items", "users"), None),
            P(("items", "users"), None),
            P(("items", "users"), None),
        ),
        check_vma=False,
    )
```

time: 248 us -> 66.2 us (0.27)
  the two profiles are of different devices: /device:TPU:0 before, /device:TPU:9 now
where the time goes in v1:
time: 66.2 us; the launch traced here: 65.8 us
  Pallas kernels  53.6 us (81%)
  local copies, waits for them, and re-layouts  9.62 us (15%)
  other arithmetic  1.34 us (2%)
  between operations  1.3 us (2%)
    pallas_call x1, Pallas kernels, on_device(): pl.pallas_call(functools.partial(kernel, n_users, n_items, edge), out_sha...  53.6 us
    unnamed x6, local copies, waits for them, and re-layouts  9.62 us
    reduce_max x1, other arithmetic, find_blocks(): return jnp.max(jnp.where(here, places[None, :], -1), axis=1)  1.34 us

profile of v1, /device:TPU:9, one launch (start us, length us, event | category | flops | bytes accessed | tf_op | source)
XLA Modules:
  0.0 65.8 jit_solution(3426563981241547202)
XLA Ops:
  1.3 1.3 %select_reduce_fusion.place = s32[192]{0:T(256)} fusion(s32[128]{0:T(128)} %bitcast.5, pred[128]{0:T(512)(128)(4,1)S(1)} %iota_compare_fusion.1), kind=kLoop, calls=%fused_computation | loop fusion | flops 98112 | bytes 1408 | tf_op jit(solution)/shard_map/reduce_max | solution.py:36
  2.6 53.6 %factorization_step.1 = (f32[512,128]{1,0:T(8,128)}, f32[512,128]{1,0:T(8,128)}, f32[512,128]{1,0:T(8,128)}, f32[192,128]{1,0:T(8,128)}, f32[192,128]{1,0:T(8,128)}, /*index=5*/f32[192,128]{1,0:T(8,128)}) custom-call(s32[192]{0:T(256)} %select_reduce_fusion.place, f32[2048,128]{1,0:T(8,128)} %uf_hbm.1, f32[2048,128]{1,0:T(8,128)} %um1_hbm.1, ...), custom_call_target="tpu_custom_call" | custom-call | tf_op jit(solution)/shard_map/factorization_step/pallas_call | solution.py:291
  56.2 1.7 %copy.22 = f32[512,128]{1,0:T(8,128)} copy(f32[512,128]{1,0:T(8,128)} %get-tuple-element.12) | data formatting | bytes 524288
  57.9 1.7 %copy.23 = f32[512,128]{1,0:T(8,128)} copy(f32[512,128]{1,0:T(8,128)} %get-tuple-element.13) | data formatting | bytes 524288
  59.5 1.7 %copy.24 = f32[512,128]{1,0:T(8,128)} copy(f32[512,128]{1,0:T(8,128)} %get-tuple-element.14) | data formatting | bytes 524288
  61.2 1.5 %copy.25 = f32[192,128]{1,0:T(8,128)} copy(f32[192,128]{1,0:T(8,128)} %get-tuple-element.15) | data formatting | bytes 196608
  62.8 1.5 %copy.26 = f32[192,128]{1,0:T(8,128)} copy(f32[192,128]{1,0:T(8,128)} %get-tuple-element.16) | data formatting | bytes 196608
  64.3 1.5 %copy.27 = f32[192,128]{1,0:T(8,128)} copy(f32[192,128]{1,0:T(8,128)} %get-tuple-element.17) | data formatting | bytes 196608
  (1 shorter events, 0.0 us)

commit v2 on v1

--- a/solution.py
+++ b/solution.py
@@ -267,6 +267,17 @@
     item_peers(lambda j: spread(j).wait_send())
     for store in stores:
         store.wait()
+
+
+def hand_out(*refs):
+    count = (len(refs) - 1) // 2
+    moves = [
+        pltpu.make_async_copy(refs[n], refs[count + n], refs[-1].at[n]) for n in range(count)
+    ]
+    for move in moves:
+        move.start()
+    for move in moves:
+        move.wait()
 
 
 def on_device(
@@ -288,9 +299,10 @@
     user_out = jax.ShapeDtypeStruct((user_share, rank), f32)
     item_out = jax.ShapeDtypeStruct((item_share, rank), f32)
     anywhere = pl.BlockSpec(memory_space=pl.ANY)
-    return pl.pallas_call(
+    out_shape = (user_out,) * 3 + (item_out,) * 3
+    results = pl.pallas_call(
         functools.partial(kernel, n_users, n_items, edge),
-        out_shape=(user_out,) * 3 + (item_out,) * 3,
+        out_shape=out_shape,
         in_specs=[pl.BlockSpec(memory_space=pltpu.SMEM)] + [anywhere] * 7,
         out_specs=(anywhere,) * 6,
         scratch_shapes=[
@@ -331,6 +343,14 @@
         place, user_factors, user_moment_one, user_moment_two,
         item_factors, item_moment_one, item_moment_two, values,
     )
+    return pl.pallas_call(
+        hand_out,
+        out_shape=out_shape,
+        in_specs=[anywhere] * 6,
+        out_specs=(anywhere,) * 6,
+        scratch_shapes=[dma((6,))],
+        name="hand_out",
+    )(*results)
 
 
 def solution(mesh):

time: 66.2 us -> 90.3 us (1.36)
  the two profiles are of different devices: /device:TPU:9 before, /device:TPU:0 now
where the time goes in v2:
time: 90.3 us; the launch traced here: 89.1 us
  Pallas kernels  86.4 us (96%)
  other arithmetic  1.34 us (1%)
  between operations  1.29 us (1%)
    pallas_call x1, Pallas kernels, on_device(): pl.pallas_call(functools.partial(kernel, n_users, n_items, edge), out_sha...  52.5 us
    pallas_call x1, Pallas kernels, on_device(): pl.pallas_call(hand_out, out_shape=out_shape, in_specs=[anywhere] * 6, ou...  33.9 us

profile of v2, /device:TPU:0, one launch (start us, length us, event | category | flops | bytes accessed | tf_op | source)
XLA Modules:
  0.0 89.1 jit_solution(9855699214152108265)
XLA Ops:
  1.3 1.3 %select_reduce_fusion.place = s32[192]{0:T(256)} fusion(s32[128]{0:T(128)} %bitcast.5, pred[128]{0:T(512)(128)(4,1)S(1)} %iota_compare_fusion.1), kind=kLoop, calls=%fused_computation | loop fusion | flops 98112 | bytes 1408 | tf_op jit(solution)/shard_map/reduce_max | solution.py:36
  2.6 52.5 %factorization_step.1 = (f32[512,128]{1,0:T(8,128)}, f32[512,128]{1,0:T(8,128)}, f32[512,128]{1,0:T(8,128)}, f32[192,128]{1,0:T(8,128)}, f32[192,128]{1,0:T(8,128)}, /*index=5*/f32[192,128]{1,0:T(8,128)}) custom-call(s32[192]{0:T(256)} %select_reduce_fusion.place, f32[2048,128]{1,0:T(8,128)} %uf_hbm.1, f32[2048,128]{1,0:T(8,128)} %um1_hbm.1, ...), custom_call_target="tpu_custom_call" | custom-call | tf_op jit(solution)/shard_map/factorization_step/pallas_call | solution.py:303
  55.1 33.9 %hand_out.1 = (f32[512,128]{1,0:T(8,128)}, f32[512,128]{1,0:T(8,128)}, f32[512,128]{1,0:T(8,128)}, f32[192,128]{1,0:T(8,128)}, f32[192,128]{1,0:T(8,128)}, /*index=5*/f32[192,128]{1,0:T(8,128)}) custom-call(f32[512,128]{1,0:T(8,128)} %get-tuple-element.12.refs_0_, f32[512,128]{1,0:T(8,128)} %get-tuple-element.13.refs_1_, ...), custom_call_target="tpu_custom_call" | custom-call | tf_op jit(solution)/shard_map/hand_out/pallas_call | solution.py:346
  (1 shorter events, 0.0 us)

commit v3 on v2

--- a/solution.py
+++ b/solution.py
@@ -41,20 +41,25 @@
     place, uf_hbm, um1_hbm, um2_hbm, if_hbm, im1_hbm, im2_hbm, vals_hbm,
     nu_hbm, nu1_hbm, nu2_hbm, ni_hbm, ni1_hbm, ni2_hbm,
     vals, uf, um1, um2, itf, im1, im2, u_low, panel, item_t,
-    acc, send_u, recv_u, new_low, item_acc, item_sum, item_send, recv_i,
-    load_sem, store_sem, gs_sem, gr_sem, us_sem, ur_sem, as_sem, ar_sem, is_sem, ir_sem,
+    new_user, part, out, in_l, in_r, new_low, item_acc, item_sum, item_send, recv_i,
+    load_sem, store_sem, gs_sem, gr_sem, us_sem, ul_sem, ur_sem, as_sem, ar_sem, is_sem, ir_sem,
 ):
     me_u, me_i = lax.axis_index("users"), lax.axis_index("items")
     user_rows, rank = uf.shape
     item_rows = panel.shape[0]
     user_share, item_share = user_rows // n_items, item_rows // n_users
-    share_blocks, item_blocks = user_share // edge, item_rows // edge
-    width = 2 if item_blocks % 2 == 0 else 1
-    pairs = item_blocks // width
+    chunks, item_blocks = user_share // edge, item_rows // edge
+    width = math.gcd(item_blocks, 4)
+    steps = item_blocks // width
     span = width * edge
+    group = math.gcd(n_items, 4)
+    group_rows = group * edge
 
     def u_share(j):
         return pl.ds(pl.multiple_of(j * user_share, user_share), user_share)
+
+    def block(j):
+        return pl.ds(pl.multiple_of(j * edge, edge), edge)
 
     def i_share(j):
         return pl.ds(pl.multiple_of(j * item_share, item_share), item_share)
@@ -121,114 +126,167 @@
 
     user_peers(lambda j: gather(j).start())
     loads[1].wait()
-    u_low[...] = uf[...].astype(bf16)
+    for c in range(chunks):
+        for j in range(n_items):
+            at = (j * chunks + c) * edge
+            u_low[c, j * edge : (j + 1) * edge, :] = uf[at : at + edge, :].astype(bf16)
     loads[2].wait()
     user_peers(lambda j: gathered(j).wait_recv())
     for b in range(item_blocks):
         item_t[:, b * edge : (b + 1) * edge] = panel[b * edge : (b + 1) * edge, :].T
 
-    def errors(rows, first_block, p):
+    def errors(rows, c, g, p):
         cols = item_t[:, pl.ds(pl.multiple_of(p * span, span), span)]
         predicted = jnp.dot(rows, cols, preferred_element_type=f32)
         strips = []
-        for ub in range(share_blocks):
+        for m in range(group):
+            user_block = (g * group + m) * chunks + c
             parts = []
             for h in range(width):
-                k = place[(first_block + ub) * item_blocks + p * width + h]
+                k = place[user_block * item_blocks + p * width + h]
                 live = jnp.where(k < 0, 0.0, 1.0).astype(f32)
                 y = vals[jnp.maximum(k, 0)].astype(f32)
-                pred = predicted[ub * edge : (ub + 1) * edge, h * edge : (h + 1) * edge]
+                pred = predicted[m * edge : (m + 1) * edge, h * edge : (h + 1) * edge]
                 parts.append(((live + (conf_alpha * live) * y) * (pred - y)).astype(bf16))
             strips.append(jnp.concatenate(parts, axis=1))
         return jnp.concatenate(strips, axis=0)
 
-    def send_share(j):
-        return to(send_u.at[j], recv_u.at[me_i], us_sem.at[j], ur_sem.at[me_i], "items", j)
-
-    def first_pass(t, carry):
-        j = lax.rem(me_i + 1 + t, n_items)
-        acc[...] = jnp.zeros_like(acc)
-
-        def step(p, c):
-            rows = u_low[u_share(j), :]
-            weighted = errors(rows, j * share_blocks, p)
-            it = panel[pl.ds(pl.multiple_of(p * span, span), span), :]
-            acc[...] += jnp.dot(weighted, it, preferred_element_type=f32)
-            return c
-
-        lax.fori_loop(0, pairs, step, 0)
-
-        @pl.when(t < n_items - 1)
+    def group_of(g):
+        return pl.ds(pl.multiple_of(g * group_rows, group_rows), group_rows)
+
+    def first_pass(c):
+        def one_group(g, carry):
+            rows = group_of(g)
+            part[c, rows, :] = jnp.zeros((group_rows, rank), f32)
+
+            def step(p, carry):
+                weighted = errors(u_low[c, rows, :], c, g, p)
+                it = panel[pl.ds(pl.multiple_of(p * span, span), span), :]
+                part[c, rows, :] += jnp.dot(weighted, it, preferred_element_type=f32)
+                return carry
+
+            return lax.fori_loop(0, steps, step, carry)
+
+        lax.fori_loop(0, n_items // group, one_group, 0)
+
+    right, left = lax.rem(me_i + 1, n_items), lax.rem(me_i + n_items - 1, n_items)
+
+    def upward(c, j):
+        return to(
+            out.at[c, block(j)], in_l.at[c, block(j)], us_sem.at[c, j], ul_sem.at[c, j],
+            "items", right,
+        )
+
+    def downward(c, j):
+        return to(
+            out.at[c, block(j)], in_r.at[c, block(j)], us_sem.at[c, j], ur_sem.at[c, j],
+            "items", left,
+        )
+
+    def add_left(c, j):
+        @pl.when(me_i > 0)
         def _():
-            send_u[j] = acc[...].astype(bf16)
-            send_share(j).start()
-
-        return carry
-
-    lax.fori_loop(0, n_items, first_pass, 0)
+            upward(c, j).wait_recv()
+            part[c, block(j), :] += in_l[c, block(j), :].astype(f32)
+
+    def add_right(c, j):
+        @pl.when(me_i < n_items - 1)
+        def _():
+            downward(c, j).wait_recv()
+            part[c, block(j), :] += in_r[c, block(j), :].astype(f32)
+
+    def send_up(c):
+        def one(t, carry):
+            j = n_items - 1 - t
+            add_left(c, j)
+            out[c, block(j), :] = part[c, block(j), :].astype(bf16)
+            upward(c, j).start()
+            return carry
+
+        lax.fori_loop(0, n_items - 1 - me_i, one, 0)
+
+    def send_down(c):
+        def one(j, carry):
+            add_right(c, j)
+            out[c, block(j), :] = part[c, block(j), :].astype(bf16)
+            downward(c, j).start()
+            return carry
+
+        lax.fori_loop(0, me_i, one, 0)
+
+    def spread(c, j):
+        mine = new_low.at[c, block(me_i)]
+        return to(mine, mine, as_sem.at[c, j], ar_sem.at[c, me_i], "items", j)
+
+    user_scale = 1.0 / math.sqrt(item_rows * n_items)
+
+    def update_users(c):
+        add_left(c, me_i)
+        add_right(c, me_i)
+        here = block(c)
+        new, one, two = adam_update(
+            uf[block(me_i * chunks + c), :], um1[here, :], um2[here, :],
+            part[c, block(me_i), :], user_scale,
+        )
+        new_low[c, block(me_i), :] = new.astype(bf16)
+        item_peers(lambda j: spread(c, j).start())
+        new_user[here, :] = new
+        um1[here, :] = one
+        um2[here, :] = two
+
+    def second_pass(c):
+        def arrived(j):
+            theirs = new_low.at[c, block(j)]
+            to(theirs, theirs, as_sem.at[c, j], ar_sem.at[c, j], "items", j).wait_recv()
+
+        item_peers(arrived)
+
+        def one_group(g, carry):
+            rows_t = jnp.concatenate(
+                [new_low[c, block(g * group + m), :].T for m in range(group)], axis=1
+            )
+
+            def step(p, carry):
+                weighted = errors(new_low[c, group_of(g), :], c, g, p)
+                cols = pl.ds(pl.multiple_of(p * span, span), span)
+                item_acc[:, cols] += jnp.dot(rows_t, weighted, preferred_element_type=f32)
+                return carry
+
+            return lax.fori_loop(0, steps, step, carry)
+
+        lax.fori_loop(0, n_items // group, one_group, 0)
+
+    item_acc[...] = jnp.zeros_like(item_acc)
     loads[3].wait()
     loads[4].wait()
-
-    def add_share(j):
-        to(
-            send_u.at[j], recv_u.at[j], us_sem.at[j], ur_sem.at[j], "items", j
-        ).wait_recv()
-        acc[...] += recv_u[j].astype(f32)
-
-    item_peers(add_share)
-    user_scale = 1.0 / math.sqrt(item_rows * n_items)
-    new, one, two = adam_update(uf[own, :], um1[...], um2[...], acc[...], user_scale)
-    new_low[own, :] = new.astype(bf16)
-
-    def spread(j):
-        mine = new_low.at[own]
-        return to(mine, mine, as_sem.at[j], ar_sem.at[me_i], "items", j)
-
-    item_peers(lambda j: spread(j).start())
-    acc[...] = new
-    um1[...] = one
-    um2[...] = two
+    below, above = me_i, n_items - 1 - me_i
+    farthest = jnp.maximum(below, above)
+
+    def stage(s, carry):
+        def at(lag, work):
+            @pl.when((s >= lag) & (s < lag + chunks))
+            def _():
+                work(s - lag)
+
+        at(0, first_pass)
+        at(below, send_up)
+        at(above, send_down)
+        at(farthest, update_users)
+        at(n_items, second_pass)
+        return carry
+
+    lax.fori_loop(0, chunks + n_items, stage, 0)
     stores = [
         pltpu.make_async_copy(src, dst, store_sem.at[n])
         for n, (src, dst) in enumerate(
             (
-                (acc, nu_hbm), (um1, nu1_hbm), (um2, nu2_hbm),
+                (new_user, nu_hbm), (um1, nu1_hbm), (um2, nu2_hbm),
                 (itf, ni_hbm), (im1, ni1_hbm), (im2, ni2_hbm),
             )
         )
     ]
     for store in stores[:3]:
         store.start()
-
-    item_acc[...] = jnp.zeros_like(item_acc)
-
-    def second_pass(t, carry):
-        j = lax.rem(me_i + t, n_items)
-
-        @pl.when(t > 0)
-        def _():
-            theirs = new_low.at[u_share(j)]
-            to(theirs, theirs, as_sem.at[j], ar_sem.at[j], "items", j).wait_recv()
-
-        rows_t = jnp.concatenate(
-            [
-                new_low[pl.ds(pl.multiple_of((j * share_blocks + b) * edge, edge), edge), :].T
-                for b in range(share_blocks)
-            ],
-            axis=1,
-        )
-
-        def step(p, c):
-            rows = new_low[u_share(j), :]
-            weighted = errors(rows, j * share_blocks, p)
-            cols = pl.ds(pl.multiple_of(p * span, span), span)
-            item_acc[:, cols] += jnp.dot(rows_t, weighted, preferred_element_type=f32)
-            return c
-
-        lax.fori_loop(0, pairs, step, 0)
-        return carry
-
-    lax.fori_loop(0, n_items, second_pass, 0)
     for b in range(item_blocks):
         tile = item_acc[:, b * edge : (b + 1) * edge].T
         item_sum[b * edge : (b + 1) * edge, :] = tile
@@ -263,21 +321,37 @@
 
     user_peers(lambda j: gather(j).wait_send())
     user_peers(lambda j: send_items(j).wait_send())
-    item_peers(lambda j: send_share(j).wait_send())
-    item_peers(lambda j: spread(j).wait_send())
+
+
+    def sent(c, carry):
+        def one(j, carry):
+            @pl.when(j != me_i)
+            def _():
+                upward(c, j).wait_send()
+                spread(c, j).wait_send()
+
+            return carry
+
+        return lax.fori_loop(0, n_items, one, carry)
+
+    lax.fori_loop(0, chunks, sent, 0)
     for store in stores:
         store.wait()
 
 
 def hand_out(*refs):
-    count = (len(refs) - 1) // 2
-    moves = [
-        pltpu.make_async_copy(refs[n], refs[count + n], refs[-1].at[n]) for n in range(count)
-    ]
-    for move in moves:
-        move.start()
-    for move in moves:
-        move.wait()
+    load_sem, store_sem = refs[-2:]
+    count = (len(refs) - 2) // 3
+    sources, targets, held = (refs[n * count : (n + 1) * count] for n in range(3))
+    loads = [pltpu.make_async_copy(sources[n], held[n], load_sem.at[n]) for n in range(count)]
+    stores = [pltpu.make_async_copy(held[n], targets[n], store_sem.at[n]) for n in range(count)]
+    for load in loads:
+        load.start()
+    for load, store in zip(loads, stores):
+        load.wait()
+        store.start()
+    for store in stores:
+        store.wait()
 
 
 def on_device(
@@ -292,6 +366,8 @@
     item_share = item_factors.shape[0]
     item_rows = item_share * n_users
     user_share = user_rows // n_items
+    chunks = user_share // edge
+    by_chunk = (chunks, n_items * edge, rank)
     slots = (user_rows // edge) * (item_rows // edge)
     place = find_blocks(block_slot[0, 0], block_count[0, 0], slots)
     vm = pltpu.VMEM
@@ -313,13 +389,15 @@
             vm((item_share, rank), f32),
             vm((item_share, rank), f32),
             vm((item_share, rank), f32),
-            vm((user_rows, rank), bf16),
+            vm(by_chunk, bf16),
             vm((item_rows, rank), bf16),
             vm((rank, item_rows), bf16),
             vm((user_share, rank), f32),
-            vm((n_items, user_share, rank), bf16),
-            vm((n_items, user_share, rank), bf16),
-            vm((user_rows, rank), bf16),
+            vm(by_chunk, f32),
+            vm(by_chunk, bf16),
+            vm(by_chunk, bf16),
+            vm(by_chunk, bf16),
+            vm(by_chunk, bf16),
             vm((rank, item_rows), f32),
             vm((item_rows, rank), f32),
             vm((item_rows, rank), bf16),
@@ -328,10 +406,11 @@
             dma((6,)),
             dma((n_users,)),
             dma((n_users,)),
-            dma((n_items,)),
-            dma((n_items,)),
-            dma((n_items,)),
-            dma((n_items,)),
+            dma((chunks, n_items)),
+            dma((chunks, n_items)),
+            dma((chunks, n_items)),
+            dma((chunks, n_items)),
+            dma((chunks, n_items)),
             dma((n_users,)),
             dma((n_users,)),
         ],
@@ -348,7 +427,7 @@
         out_shape=out_shape,
         in_specs=[anywhere] * 6,
         out_specs=(anywhere,) * 6,
-        scratch_shapes=[dma((6,))],
+        scratch_shapes=[vm(o.shape, f32) for o in out_shape] + [dma((6,)), dma((6,))],
         name="hand_out",
     )(*results)
 

time: 90.3 us -> 51.2 us (0.57); the launches traced: 89.1 us -> 51 us
  Pallas kernels: 86.4 us -> 48.4 us
    pallas_call x1, Pallas kernels: 33.9 us -> 2.02 us  [on_device(): pl.pallas_call(hand_out, out_shape=out_shape, in_specs=[anywhere] * 6, ou...]
    pallas_call x1, Pallas kernels: 52.5 us -> 46.4 us  [on_device(): pl.pallas_call(functools.partial(kernel, n_users, n_items, edge), out_sha...]
where the time goes in v3:
time: 51.2 us; the launch traced here: 51 us
  Pallas kernels  48.4 us (95%)
  other arithmetic  1.34 us (3%)
  between operations  1.29 us (3%)
    pallas_call x1, Pallas kernels, on_device(): pl.pallas_call(functools.partial(kernel, n_users, n_items, edge), out_sha...  46.4 us
    pallas_call x1, Pallas kernels, on_device(): pl.pallas_call(hand_out, out_shape=out_shape, in_specs=[anywhere] * 6, ou...  2.02 us
    reduce_max x1, other arithmetic, find_blocks(): return jnp.max(jnp.where(here, places[None, :], -1), axis=1)  1.34 us

profile of v3, /device:TPU:0, one launch (start us, length us, event | category | flops | bytes accessed | tf_op | source)
XLA Modules:
  0.0 51.0 jit_solution(11487996991297843188)
XLA Ops:
  1.3 1.3 %select_reduce_fusion.place = s32[192]{0:T(256)} fusion(s32[128]{0:T(128)} %bitcast.5, pred[128]{0:T(512)(128)(4,1)S(1)} %iota_compare_fusion.1), kind=kLoop, calls=%fused_computation | loop fusion | flops 98112 | bytes 1408 | tf_op jit(solution)/shard_map/reduce_max | solution.py:36
  2.6 46.4 %factorization_step.1 = (f32[512,128]{1,0:T(8,128)}, f32[512,128]{1,0:T(8,128)}, f32[512,128]{1,0:T(8,128)}, f32[192,128]{1,0:T(8,128)}, f32[192,128]{1,0:T(8,128)}, /*index=5*/f32[192,128]{1,0:T(8,128)}) custom-call(s32[192]{0:T(256)} %select_reduce_fusion.place, f32[2048,128]{1,0:T(8,128)} %uf_hbm.1, f32[2048,128]{1,0:T(8,128)} %um1_hbm.1, ...), custom_call_target="tpu_custom_call" | custom-call | tf_op jit(solution)/shard_map/factorization_step/pallas_call | solution.py:379
  49.0 2.0 %hand_out.1 = (f32[512,128]{1,0:T(8,128)}, f32[512,128]{1,0:T(8,128)}, f32[512,128]{1,0:T(8,128)}, f32[192,128]{1,0:T(8,128)}, f32[192,128]{1,0:T(8,128)}, /*index=5*/f32[192,128]{1,0:T(8,128)}) custom-call(f32[512,128]{1,0:T(8,128)} %get-tuple-element.12.refs_0_, f32[512,128]{1,0:T(8,128)} %get-tuple-element.13.refs_1_, ...), custom_call_target="tpu_custom_call" | custom-call | tf_op jit(solution)/shard_map/hand_out/pallas_call | solution.py:425
  (1 shorter events, 0.0 us)

commit v4 on v3

--- a/solution.py
+++ b/solution.py
@@ -41,7 +41,7 @@
     place, uf_hbm, um1_hbm, um2_hbm, if_hbm, im1_hbm, im2_hbm, vals_hbm,
     nu_hbm, nu1_hbm, nu2_hbm, ni_hbm, ni1_hbm, ni2_hbm,
     vals, uf, um1, um2, itf, im1, im2, u_low, panel, item_t,
-    new_user, part, out, in_l, in_r, new_low, item_acc, item_sum, item_send, recv_i,
+    new_user, part, out, in_l, in_r, new_low, new_t, item_acc, item_sum, item_send, recv_i,
     load_sem, store_sem, gs_sem, gr_sem, us_sem, ul_sem, ur_sem, as_sem, ar_sem, is_sem, ir_sem,
 ):
     me_u, me_i = lax.axis_index("users"), lax.axis_index("items")
@@ -49,9 +49,11 @@
     item_rows = panel.shape[0]
     user_share, item_share = user_rows // n_items, item_rows // n_users
     chunks, item_blocks = user_share // edge, item_rows // edge
-    width = math.gcd(item_blocks, 4)
-    steps = item_blocks // width
+    width = math.gcd(item_blocks, 2)
     span = width * edge
+    halves = 2 if n_users % 2 == 0 and (item_blocks // width) % 2 == 0 else 1
+    steps = item_blocks // width // halves
+    half_shares, half_blocks = n_users // halves, item_blocks // halves
     group = math.gcd(n_items, 4)
     group_rows = group * edge
 
@@ -135,9 +137,13 @@
     for b in range(item_blocks):
         item_t[:, b * edge : (b + 1) * edge] = panel[b * edge : (b + 1) * edge, :].T
 
-    def errors(rows, c, g, p):
-        cols = item_t[:, pl.ds(pl.multiple_of(p * span, span), span)]
-        predicted = jnp.dot(rows, cols, preferred_element_type=f32)
+    def span_of(p):
+        return pl.ds(pl.multiple_of(p * span, span), span)
+
+    def predict(rows, p):
+        return jnp.dot(rows, item_t[:, span_of(p)], preferred_element_type=f32)
+
+    def errors(predicted, c, g, p):
         strips = []
         for m in range(group):
             user_block = (g * group + m) * chunks + c
@@ -151,6 +157,15 @@
             strips.append(jnp.concatenate(parts, axis=1))
         return jnp.concatenate(strips, axis=0)
 
+    def sweep(rows, c, g, half, use):
+        first = half * steps
+        ahead = predict(rows, first)
+        for q in range(steps):
+            predicted = ahead
+            if q < steps - 1:
+                ahead = predict(rows, first + q + 1)
+            use(errors(predicted, c, g, first + q), first + q)
+
     def group_of(g):
         return pl.ds(pl.multiple_of(g * group_rows, group_rows), group_rows)
 
@@ -159,13 +174,16 @@
             rows = group_of(g)
             part[c, rows, :] = jnp.zeros((group_rows, rank), f32)
 
-            def step(p, carry):
-                weighted = errors(u_low[c, rows, :], c, g, p)
-                it = panel[pl.ds(pl.multiple_of(p * span, span), span), :]
-                part[c, rows, :] += jnp.dot(weighted, it, preferred_element_type=f32)
+            def one_half(half, carry):
+                def use(weighted, p):
+                    part[c, rows, :] += jnp.dot(
+                        weighted, panel[span_of(p), :], preferred_element_type=f32
+                    )
+
+                sweep(u_low[c, rows, :], c, g, half, use)
                 return carry
 
-            return lax.fori_loop(0, steps, step, carry)
+            return lax.fori_loop(0, halves, one_half, carry)
 
         lax.fori_loop(0, n_items // group, one_group, 0)
 
@@ -241,20 +259,56 @@
 
         item_peers(arrived)
 
-        def one_group(g, carry):
-            rows_t = jnp.concatenate(
-                [new_low[c, block(g * group + m), :].T for m in range(group)], axis=1
-            )
-
-            def step(p, carry):
-                weighted = errors(new_low[c, group_of(g), :], c, g, p)
-                cols = pl.ds(pl.multiple_of(p * span, span), span)
-                item_acc[:, cols] += jnp.dot(rows_t, weighted, preferred_element_type=f32)
+        for j in range(n_items):
+            new_t[:, j * edge : (j + 1) * edge] = new_low[c, j * edge : (j + 1) * edge, :].T
+
+        def one_half(t, carry):
+            half = lax.rem(me_u // half_shares + 1 + t, halves)
+
+            def one_group(g, carry):
+                rows_t = new_t[:, group_of(g)]
+
+                def use(weighted, p):
+                    item_acc[:, span_of(p)] += jnp.dot(
+                        rows_t, weighted, preferred_element_type=f32
+                    )
+
+                sweep(new_low[c, group_of(g), :], c, g, half, use)
                 return carry
 
-            return lax.fori_loop(0, steps, step, carry)
-
-        lax.fori_loop(0, n_items // group, one_group, 0)
+            lax.fori_loop(0, n_items // group, one_group, 0)
+
+            @pl.when(c == chunks - 1)
+            def _():
+                send_half(half)
+
+            return carry
+
+        lax.fori_loop(0, halves, one_half, 0)
+
+    def send_items(j):
+        return to(
+            item_send.at[i_share(j)], recv_i.at[me_u],
+            is_sem.at[j], ir_sem.at[me_u], "users", j,
+        )
+
+    def send_half(half):
+        for b in range(half_blocks):
+            at = block(half * half_blocks + b)
+            tile = item_acc[:, at].T
+            item_sum[at, :] = tile
+            item_send[at, :] = tile.astype(bf16)
+
+        def one(t, carry):
+            j = half * half_shares + lax.rem(me_u + 1 + t, half_shares)
+
+            @pl.when(j != me_u)
+            def _():
+                send_items(j).start()
+
+            return carry
+
+        lax.fori_loop(0, half_shares, one, 0)
 
     item_acc[...] = jnp.zeros_like(item_acc)
     loads[3].wait()
@@ -287,18 +341,6 @@
     ]
     for store in stores[:3]:
         store.start()
-    for b in range(item_blocks):
-        tile = item_acc[:, b * edge : (b + 1) * edge].T
-        item_sum[b * edge : (b + 1) * edge, :] = tile
-        item_send[b * edge : (b + 1) * edge, :] = tile.astype(bf16)
-
-    def send_items(j):
-        return to(
-            item_send.at[i_share(j)], recv_i.at[me_u],
-            is_sem.at[j], ir_sem.at[me_u], "users", j,
-        )
-
-    user_peers(lambda j: send_items(j).start())
     loads[5].wait()
     loads[6].wait()
 
@@ -398,6 +440,7 @@
             vm(by_chunk, bf16),
             vm(by_chunk, bf16),
             vm(by_chunk, bf16),
+            vm((rank, n_items * edge), bf16),
             vm((rank, item_rows), f32),
             vm((item_rows, rank), f32),
             vm((item_rows, rank), bf16),

time: 51.2 us -> 50.5 us (0.986)
  Pallas kernels: 48.4 us -> 47.6 us
    pallas_call x1, Pallas kernels: 46.4 us -> 45.6 us  [on_device(): pl.pallas_call(functools.partial(kernel, n_users, n_items, edge), out_sha...]
where the time goes in v4:
time: 50.5 us; the launch traced here: 50.3 us
  Pallas kernels  47.6 us (94%)
  other arithmetic  1.34 us (3%)
  between operations  1.29 us (3%)
    pallas_call x1, Pallas kernels, on_device(): pl.pallas_call(functools.partial(kernel, n_users, n_items, edge), out_sha...  45.6 us
    pallas_call x1, Pallas kernels, on_device(): pl.pallas_call(hand_out, out_shape=out_shape, in_specs=[anywhere] * 6, ou...  2.02 us
    reduce_max x1, other arithmetic, find_blocks(): return jnp.max(jnp.where(here, places[None, :], -1), axis=1)  1.34 us

profile of v4, /device:TPU:0, one launch (start us, length us, event | category | flops | bytes accessed | tf_op | source)
XLA Modules:
  0.0 50.3 jit_solution(4705724825246146107)
XLA Ops:
  1.3 1.3 %select_reduce_fusion.place = s32[192]{0:T(256)} fusion(s32[128]{0:T(128)} %bitcast.5, pred[128]{0:T(512)(128)(4,1)S(1)} %iota_compare_fusion.1), kind=kLoop, calls=%fused_computation | loop fusion | flops 98112 | bytes 1408 | tf_op jit(solution)/shard_map/reduce_max | solution.py:36
  2.6 45.6 %factorization_step.1 = (f32[512,128]{1,0:T(8,128)}, f32[512,128]{1,0:T(8,128)}, f32[512,128]{1,0:T(8,128)}, f32[192,128]{1,0:T(8,128)}, f32[192,128]{1,0:T(8,128)}, /*index=5*/f32[192,128]{1,0:T(8,128)}) custom-call(s32[192]{0:T(256)} %select_reduce_fusion.place, f32[2048,128]{1,0:T(8,128)} %uf_hbm.1, f32[2048,128]{1,0:T(8,128)} %um1_hbm.1, ...), custom_call_target="tpu_custom_call" | custom-call | tf_op jit(solution)/shard_map/factorization_step/pallas_call | solution.py:421
  48.3 2.0 %hand_out.1 = (f32[512,128]{1,0:T(8,128)}, f32[512,128]{1,0:T(8,128)}, f32[512,128]{1,0:T(8,128)}, f32[192,128]{1,0:T(8,128)}, f32[192,128]{1,0:T(8,128)}, /*index=5*/f32[192,128]{1,0:T(8,128)}) custom-call(f32[512,128]{1,0:T(8,128)} %get-tuple-element.12.refs_0_, f32[512,128]{1,0:T(8,128)} %get-tuple-element.13.refs_1_, ...), custom_call_target="tpu_custom_call" | custom-call | tf_op jit(solution)/shard_map/hand_out/pallas_call | solution.py:468
  (1 shorter events, 0.0 us)

commit v5 on v4

--- a/solution.py
+++ b/solution.py
@@ -42,7 +42,7 @@
     nu_hbm, nu1_hbm, nu2_hbm, ni_hbm, ni1_hbm, ni2_hbm,
     vals, uf, um1, um2, itf, im1, im2, u_low, panel, item_t,
     new_user, part, out, in_l, in_r, new_low, new_t, item_acc, item_sum, item_send, recv_i,
-    load_sem, store_sem, gs_sem, gr_sem, us_sem, ul_sem, ur_sem, as_sem, ar_sem, is_sem, ir_sem,
+    load_sem, store_sem, gs_sem, gr_sem, us_sem, ul_sem, ur_sem, au_sem, ad_sem, ar_sem, is_sem, ir_sem,
 ):
     me_u, me_i = lax.axis_index("users"), lax.axis_index("items")
     user_rows, rank = uf.shape
@@ -232,9 +232,38 @@
 
         lax.fori_loop(0, me_i, one, 0)
 
-    def spread(c, j):
-        mine = new_low.at[c, block(me_i)]
-        return to(mine, mine, as_sem.at[c, j], ar_sem.at[c, me_i], "items", j)
+    def pass_up(c, j):
+        it = new_low.at[c, block(j)]
+        return to(it, it, au_sem.at[c, j], ar_sem.at[c, j], "items", right)
+
+    def pass_down(c, j):
+        it = new_low.at[c, block(j)]
+        return to(it, it, ad_sem.at[c, j], ar_sem.at[c, j], "items", left)
+
+    def pass_on(c, d):
+        @pl.when((me_i - d >= 0) & (me_i < n_items - 1))
+        def _():
+            pass_up(c, me_i - d).wait_recv()
+            pass_up(c, me_i - d).start()
+
+        @pl.when((me_i + d < n_items) & (me_i > 0))
+        def _():
+            pass_down(c, me_i + d).wait_recv()
+            pass_down(c, me_i + d).start()
+
+    def pass_on_far(c):
+        def one(d, carry):
+            pass_on(c, d)
+            return carry
+
+        lax.fori_loop(2, n_items, one, 0)
+
+    def pass_on_near(c):
+        pass_on(c, 1)
+
+        @pl.when(c == 0)
+        def _():
+            pass_on_far(c)
 
     user_scale = 1.0 / math.sqrt(item_rows * n_items)
 
@@ -247,15 +276,24 @@
             part[c, block(me_i), :], user_scale,
         )
         new_low[c, block(me_i), :] = new.astype(bf16)
-        item_peers(lambda j: spread(c, j).start())
+
+        @pl.when(me_i < n_items - 1)
+        def _():
+            pass_up(c, me_i).start()
+
+        @pl.when(me_i > 0)
+        def _():
+            pass_down(c, me_i).start()
+
         new_user[here, :] = new
         um1[here, :] = one
         um2[here, :] = two
 
     def second_pass(c):
         def arrived(j):
-            theirs = new_low.at[c, block(j)]
-            to(theirs, theirs, as_sem.at[c, j], ar_sem.at[c, j], "items", j).wait_recv()
+            @pl.when((me_i == 0) | (me_i == n_items - 1))
+            def _():
+                pass_up(c, j).wait_recv()
 
         item_peers(arrived)
 
@@ -277,6 +315,10 @@
                 return carry
 
             lax.fori_loop(0, n_items // group, one_group, 0)
+
+            @pl.when((t == 0) & (c < chunks - 1))
+            def _():
+                pass_on_far(c + 1)
 
             @pl.when(c == chunks - 1)
             def _():
@@ -326,10 +368,11 @@
         at(below, send_up)
         at(above, send_down)
         at(farthest, update_users)
-        at(n_items, second_pass)
+        at(n_items, pass_on_near)
+        at(n_items + 1, second_pass)
         return carry
 
-    lax.fori_loop(0, chunks + n_items, stage, 0)
+    lax.fori_loop(0, chunks + n_items + 1, stage, 0)
     stores = [
         pltpu.make_async_copy(src, dst, store_sem.at[n])
         for n, (src, dst) in enumerate(
@@ -370,7 +413,14 @@
             @pl.when(j != me_i)
             def _():
                 upward(c, j).wait_send()
-                spread(c, j).wait_send()
+
+            @pl.when((j <= me_i) & (me_i < n_items - 1))
+            def _():
+                pass_up(c, j).wait_send()
+
+            @pl.when((j >= me_i) & (me_i > 0))
+            def _():
+                pass_down(c, j).wait_send()
 
             return carry
 
@@ -454,6 +504,7 @@
             dma((chunks, n_items)),
             dma((chunks, n_items)),
             dma((chunks, n_items)),
+            dma((chunks, n_items)),
             dma((n_users,)),
             dma((n_users,)),
         ],

time: 50.5 us -> 54.6 us (1.081)
  Pallas kernels: 47.6 us -> 51.8 us
    pallas_call x1, Pallas kernels: 45.6 us -> 49.8 us  [on_device(): pl.pallas_call(functools.partial(kernel, n_users, n_items, edge), out_sha...]
where the time goes in v5:
time: 54.6 us; the launch traced here: 54.5 us
  Pallas kernels  51.8 us (95%)
  other arithmetic  1.34 us (2%)
  between operations  1.29 us (2%)
    pallas_call x1, Pallas kernels, on_device(): pl.pallas_call(functools.partial(kernel, n_users, n_items, edge), out_sha...  49.8 us
    pallas_call x1, Pallas kernels, on_device(): pl.pallas_call(hand_out, out_shape=out_shape, in_specs=[anywhere] * 6, ou...  2.02 us
    reduce_max x1, other arithmetic, find_blocks(): return jnp.max(jnp.where(here, places[None, :], -1), axis=1)  1.34 us

profile of v5, /device:TPU:0, one launch (start us, length us, event | category | flops | bytes accessed | tf_op | source)
XLA Modules:
  0.0 54.5 jit_solution(2924615260974089065)
XLA Ops:
  1.3 1.3 %select_reduce_fusion.place = s32[192]{0:T(256)} fusion(s32[128]{0:T(128)} %bitcast.5, pred[128]{0:T(512)(128)(4,1)S(1)} %iota_compare_fusion.1), kind=kLoop, calls=%fused_computation | loop fusion | flops 98112 | bytes 1408 | tf_op jit(solution)/shard_map/reduce_max | solution.py:36
  2.6 49.8 %factorization_step.1 = (f32[512,128]{1,0:T(8,128)}, f32[512,128]{1,0:T(8,128)}, f32[512,128]{1,0:T(8,128)}, f32[192,128]{1,0:T(8,128)}, f32[192,128]{1,0:T(8,128)}, /*index=5*/f32[192,128]{1,0:T(8,128)}) custom-call(s32[192]{0:T(256)} %select_reduce_fusion.place, f32[2048,128]{1,0:T(8,128)} %uf_hbm.1, f32[2048,128]{1,0:T(8,128)} %um1_hbm.1, ...), custom_call_target="tpu_custom_call" | custom-call | tf_op jit(solution)/shard_map/factorization_step/pallas_call | solution.py:471
  52.4 2.0 %hand_out.1 = (f32[512,128]{1,0:T(8,128)}, f32[512,128]{1,0:T(8,128)}, f32[512,128]{1,0:T(8,128)}, f32[192,128]{1,0:T(8,128)}, f32[192,128]{1,0:T(8,128)}, /*index=5*/f32[192,128]{1,0:T(8,128)}) custom-call(f32[512,128]{1,0:T(8,128)} %get-tuple-element.12.refs_0_, f32[512,128]{1,0:T(8,128)} %get-tuple-element.13.refs_1_, ...), custom_call_target="tpu_custom_call" | custom-call | tf_op jit(solution)/shard_map/hand_out/pallas_call | solution.py:519
  (1 shorter events, 0.0 us)

commit v6 on v4

--- a/solution.py
+++ b/solution.py
@@ -41,8 +41,8 @@
     place, uf_hbm, um1_hbm, um2_hbm, if_hbm, im1_hbm, im2_hbm, vals_hbm,
     nu_hbm, nu1_hbm, nu2_hbm, ni_hbm, ni1_hbm, ni2_hbm,
     vals, uf, um1, um2, itf, im1, im2, u_low, panel, item_t,
-    new_user, part, out, in_l, in_r, new_low, new_t, item_acc, item_sum, item_send, recv_i,
-    load_sem, store_sem, gs_sem, gr_sem, us_sem, ul_sem, ur_sem, as_sem, ar_sem, is_sem, ir_sem,
+    new_user, part, out, taken, new_low, new_t, item_acc, item_sum, item_send, recv_i,
+    load_sem, store_sem, gs_sem, gr_sem, us_sem, ur_sem, as_sem, ar_sem, is_sem, ir_sem,
 ):
     me_u, me_i = lax.axis_index("users"), lax.axis_index("items")
     user_rows, rank = uf.shape
@@ -187,50 +187,18 @@
 
         lax.fori_loop(0, n_items // group, one_group, 0)
 
-    right, left = lax.rem(me_i + 1, n_items), lax.rem(me_i + n_items - 1, n_items)
-
-    def upward(c, j):
+    def send_part(c, j):
         return to(
-            out.at[c, block(j)], in_l.at[c, block(j)], us_sem.at[c, j], ul_sem.at[c, j],
-            "items", right,
-        )
-
-    def downward(c, j):
-        return to(
-            out.at[c, block(j)], in_r.at[c, block(j)], us_sem.at[c, j], ur_sem.at[c, j],
-            "items", left,
-        )
-
-    def add_left(c, j):
-        @pl.when(me_i > 0)
-        def _():
-            upward(c, j).wait_recv()
-            part[c, block(j), :] += in_l[c, block(j), :].astype(f32)
-
-    def add_right(c, j):
-        @pl.when(me_i < n_items - 1)
-        def _():
-            downward(c, j).wait_recv()
-            part[c, block(j), :] += in_r[c, block(j), :].astype(f32)
-
-    def send_up(c):
-        def one(t, carry):
-            j = n_items - 1 - t
-            add_left(c, j)
+            out.at[c, block(j)], taken.at[c, block(me_i)], us_sem.at[c, j], ur_sem.at[c, me_i],
+            "items", j,
+        )
+
+    def send_parts(c):
+        def one(j):
             out[c, block(j), :] = part[c, block(j), :].astype(bf16)
-            upward(c, j).start()
-            return carry
-
-        lax.fori_loop(0, n_items - 1 - me_i, one, 0)
-
-    def send_down(c):
-        def one(j, carry):
-            add_right(c, j)
-            out[c, block(j), :] = part[c, block(j), :].astype(bf16)
-            downward(c, j).start()
-            return carry
-
-        lax.fori_loop(0, me_i, one, 0)
+            send_part(c, j).start()
+
+        item_peers(one)
 
     def spread(c, j):
         mine = new_low.at[c, block(me_i)]
@@ -239,8 +207,14 @@
     user_scale = 1.0 / math.sqrt(item_rows * n_items)
 
     def update_users(c):
-        add_left(c, me_i)
-        add_right(c, me_i)
+        def add_part(j):
+            to(
+                out.at[c, block(j)], taken.at[c, block(j)], us_sem.at[c, j], ur_sem.at[c, j],
+                "items", j,
+            ).wait_recv()
+            part[c, block(me_i), :] += taken[c, block(j), :].astype(f32)
+
+        item_peers(add_part)
         here = block(c)
         new, one, two = adam_update(
             uf[block(me_i * chunks + c), :], um1[here, :], um2[here, :],
@@ -313,8 +287,6 @@
     item_acc[...] = jnp.zeros_like(item_acc)
     loads[3].wait()
     loads[4].wait()
-    below, above = me_i, n_items - 1 - me_i
-    farthest = jnp.maximum(below, above)
 
     def stage(s, carry):
         def at(lag, work):
@@ -323,13 +295,12 @@
                 work(s - lag)
 
         at(0, first_pass)
-        at(below, send_up)
-        at(above, send_down)
-        at(farthest, update_users)
-        at(n_items, second_pass)
+        at(0, send_parts)
+        at(1, update_users)
+        at(3, second_pass)
         return carry
 
-    lax.fori_loop(0, chunks + n_items, stage, 0)
+    lax.fori_loop(0, chunks + 3, stage, 0)
     stores = [
         pltpu.make_async_copy(src, dst, store_sem.at[n])
         for n, (src, dst) in enumerate(
@@ -369,7 +340,7 @@
         def one(j, carry):
             @pl.when(j != me_i)
             def _():
-                upward(c, j).wait_send()
+                send_part(c, j).wait_send()
                 spread(c, j).wait_send()
 
             return carry
@@ -439,7 +410,6 @@
             vm(by_chunk, bf16),
             vm(by_chunk, bf16),
             vm(by_chunk, bf16),
-            vm(by_chunk, bf16),
             vm((rank, n_items * edge), bf16),
             vm((rank, item_rows), f32),
             vm((item_rows, rank), f32),
@@ -449,7 +419,6 @@
             dma((6,)),
             dma((n_users,)),
             dma((n_users,)),
-            dma((chunks, n_items)),
             dma((chunks, n_items)),
             dma((chunks, n_items)),
             dma((chunks, n_items)),

time: 50.5 us -> 50.7 us (level)
  no operation moved by 1% of the time
where the time goes in v6:
time: 50.7 us; the launch traced here: 50.5 us
  Pallas kernels  47.9 us (94%)
  other arithmetic  1.34 us (3%)
  between operations  1.29 us (3%)
    pallas_call x1, Pallas kernels, on_device(): pl.pallas_call(functools.partial(kernel, n_users, n_items, edge), out_sha...  45.9 us
    pallas_call x1, Pallas kernels, on_device(): pl.pallas_call(hand_out, out_shape=out_shape, in_specs=[anywhere] * 6, ou...  2.02 us
    reduce_max x1, other arithmetic, find_blocks(): return jnp.max(jnp.where(here, places[None, :], -1), axis=1)  1.34 us

profile of v6, /device:TPU:0, one launch (start us, length us, event | category | flops | bytes accessed | tf_op | source)
XLA Modules:
  0.0 50.5 jit_solution(2347626060330391467)
XLA Ops:
  1.3 1.3 %select_reduce_fusion.place = s32[192]{0:T(256)} fusion(s32[128]{0:T(128)} %bitcast.5, pred[128]{0:T(512)(128)(4,1)S(1)} %iota_compare_fusion.1), kind=kLoop, calls=%fused_computation | loop fusion | flops 98112 | bytes 1408 | tf_op jit(solution)/shard_map/reduce_max | solution.py:36
  2.6 45.9 %factorization_step.1 = (f32[512,128]{1,0:T(8,128)}, f32[512,128]{1,0:T(8,128)}, f32[512,128]{1,0:T(8,128)}, f32[192,128]{1,0:T(8,128)}, f32[192,128]{1,0:T(8,128)}, /*index=5*/f32[192,128]{1,0:T(8,128)}) custom-call(s32[192]{0:T(256)} %select_reduce_fusion.place, f32[2048,128]{1,0:T(8,128)} %uf_hbm.1, f32[2048,128]{1,0:T(8,128)} %um1_hbm.1, ...), custom_call_target="tpu_custom_call" | custom-call | tf_op jit(solution)/shard_map/factorization_step/pallas_call | solution.py:392
  48.5 2.0 %hand_out.1 = (f32[512,128]{1,0:T(8,128)}, f32[512,128]{1,0:T(8,128)}, f32[512,128]{1,0:T(8,128)}, f32[192,128]{1,0:T(8,128)}, f32[192,128]{1,0:T(8,128)}, /*index=5*/f32[192,128]{1,0:T(8,128)}) custom-call(f32[512,128]{1,0:T(8,128)} %get-tuple-element.12.refs_0_, f32[512,128]{1,0:T(8,128)} %get-tuple-element.13.refs_1_, ...), custom_call_target="tpu_custom_call" | custom-call | tf_op jit(solution)/shard_map/hand_out/pallas_call | solution.py:437
  (1 shorter events, 0.0 us)

commit v7 on v6

--- a/solution.py
+++ b/solution.py
@@ -42,7 +42,7 @@
     nu_hbm, nu1_hbm, nu2_hbm, ni_hbm, ni1_hbm, ni2_hbm,
     vals, uf, um1, um2, itf, im1, im2, u_low, panel, item_t,
     new_user, part, out, taken, new_low, new_t, item_acc, item_sum, item_send, recv_i,
-    load_sem, store_sem, gs_sem, gr_sem, us_sem, ur_sem, as_sem, ar_sem, is_sem, ir_sem,
+    load_sem, value_sem, store_sem, gs_sem, gr_sem, us_sem, ur_sem, as_sem, ar_sem, is_sem, ir_sem,
 ):
     me_u, me_i = lax.axis_index("users"), lax.axis_index("items")
     user_rows, rank = uf.shape
@@ -91,13 +91,23 @@
         pltpu.make_async_copy(src, dst, load_sem.at[n])
         for n, (src, dst) in enumerate(
             (
-                (if_hbm, itf), (uf_hbm, uf), (vals_hbm, vals),
+                (if_hbm, itf), (uf_hbm, uf), (im1_hbm, im1),
                 (um1_hbm.at[own], um1), (um2_hbm.at[own], um2),
-                (im1_hbm, im1), (im2_hbm, im2),
+                (im2_hbm, im2),
             )
         )
     ]
-    for load in loads:
+    pieces = math.gcd(vals.shape[0], 16)
+    piece = vals.shape[0] // pieces
+    value_loads = [
+        pltpu.make_async_copy(
+            vals_hbm.at[n * piece : (n + 1) * piece],
+            vals.at[n * piece : (n + 1) * piece],
+            value_sem.at[n],
+        )
+        for n in range(pieces)
+    ]
+    for load in loads[:2] + value_loads + loads[2:]:
         load.start()
 
     barrier = pltpu.get_barrier_semaphore()
@@ -132,10 +142,11 @@
         for j in range(n_items):
             at = (j * chunks + c) * edge
             u_low[c, j * edge : (j + 1) * edge, :] = uf[at : at + edge, :].astype(bf16)
-    loads[2].wait()
     user_peers(lambda j: gathered(j).wait_recv())
     for b in range(item_blocks):
         item_t[:, b * edge : (b + 1) * edge] = panel[b * edge : (b + 1) * edge, :].T
+    for load in value_loads:
+        load.wait()
 
     def span_of(p):
         return pl.ds(pl.multiple_of(p * span, span), span)
@@ -312,8 +323,8 @@
     ]
     for store in stores[:3]:
         store.start()
+    loads[2].wait()
     loads[5].wait()
-    loads[6].wait()
 
     def add_items(j):
         to(
@@ -415,7 +426,8 @@
             vm((item_rows, rank), f32),
             vm((item_rows, rank), bf16),
             vm((n_users, item_share, rank), bf16),
-            dma((7,)),
+            dma((6,)),
+            dma((math.gcd(values.shape[0], 16),)),
             dma((6,)),
             dma((n_users,)),
             dma((n_users,)),

time: 50.7 us -> 51 us (level)
  no operation moved by 1% of the time
where the time goes in v7:
time: 51 us; the launch traced here: 50.8 us
  Pallas kernels  48.2 us (95%)
  other arithmetic  1.34 us (3%)
  between operations  1.29 us (3%)
    pallas_call x1, Pallas kernels, on_device(): pl.pallas_call(functools.partial(kernel, n_users, n_items, edge), out_sha...  46.1 us
    pallas_call x1, Pallas kernels, on_device(): pl.pallas_call(hand_out, out_shape=out_shape, in_specs=[anywhere] * 6, ou...  2.02 us
    reduce_max x1, other arithmetic, find_blocks(): return jnp.max(jnp.where(here, places[None, :], -1), axis=1)  1.34 us

profile of v7, /device:TPU:0, one launch (start us, length us, event | category | flops | bytes accessed | tf_op | source)
XLA Modules:
  0.0 50.8 jit_solution(2084411505273192167)
XLA Ops:
  1.3 1.3 %select_reduce_fusion.place = s32[192]{0:T(256)} fusion(s32[128]{0:T(128)} %bitcast.5, pred[128]{0:T(512)(128)(4,1)S(1)} %iota_compare_fusion.1), kind=kLoop, calls=%fused_computation | loop fusion | flops 98112 | bytes 1408 | tf_op jit(solution)/shard_map/reduce_max | solution.py:36
  2.6 46.1 %factorization_step.1 = (f32[512,128]{1,0:T(8,128)}, f32[512,128]{1,0:T(8,128)}, f32[512,128]{1,0:T(8,128)}, f32[192,128]{1,0:T(8,128)}, f32[192,128]{1,0:T(8,128)}, /*index=5*/f32[192,128]{1,0:T(8,128)}) custom-call(s32[192]{0:T(256)} %select_reduce_fusion.place, f32[2048,128]{1,0:T(8,128)} %uf_hbm.1, f32[2048,128]{1,0:T(8,128)} %um1_hbm.1, ...), custom_call_target="tpu_custom_call" | custom-call | tf_op jit(solution)/shard_map/factorization_step/pallas_call | solution.py:403
  48.8 2.0 %hand_out.1 = (f32[512,128]{1,0:T(8,128)}, f32[512,128]{1,0:T(8,128)}, f32[512,128]{1,0:T(8,128)}, f32[192,128]{1,0:T(8,128)}, f32[192,128]{1,0:T(8,128)}, /*index=5*/f32[192,128]{1,0:T(8,128)}) custom-call(f32[512,128]{1,0:T(8,128)} %get-tuple-element.12.refs_0_, f32[512,128]{1,0:T(8,128)} %get-tuple-element.13.refs_1_, ...), custom_call_target="tpu_custom_call" | custom-call | tf_op jit(solution)/shard_map/hand_out/pallas_call | solution.py:449
  (1 shorter events, 0.0 us)
